TPU v7x, 512 devices: a whole 4x8x8 slice. The times are simulated.
512 devices in a mesh: outer: 16 (over z_lo, x), inner: 32 (over y, z_hi, core).
Axes of the slice: x: 4, y: 8, z: 8 (z_hi: 2, z_lo: 4; z = z_hi * 4 + z_lo), core: 2. Of those that a mesh axis runs over, the one named last changes fastest.
Arguments:
- queries: bfloat16 [65536, 128], P(('outer', 'inner')), may hold values from -6 to 6
- keys: bfloat16 [65536, 128], P(('outer', 'inner')), may hold values from -6 to 6
- values: bfloat16 [65536, 128], P(('outer', 'inner')), may hold values from -6 to 6
- attended: bfloat16 [65536, 128], P(('outer', 'inner')), may hold values from -3 to 3
- out_grad: bfloat16 [65536, 128], P(('outer', 'inner')), may hold values from -384 to 384
- logsumexp: float32 [65536], P(('outer', 'inner')), may hold values from 10 to 11.5
Outputs:
- query_grad: bfloat16 [65536, 128], P(('outer', 'inner'))
- key_grad: bfloat16 [65536, 128], P(('outer', 'inner'))
- value_grad: bfloat16 [65536, 128], P(('outer', 'inner'))
All inputs are finite; a program needn't handle non-finite values.
Results may differ from a plain program's by a relative error of at most 0.008.
Values may be sent and summed in bfloat16 or wider, within the bound.
A program may use at most 64 MiB of HBM per device.

v0:
```python
import jax
import jax.numpy as jnp
from jax import lax
from jax.sharding import PartitionSpec as P


def tile_grads(qrow, grow, stat_rows, key_all, val_all, scale):
    scores = jnp.dot(qrow, key_all.T, preferred_element_type=jnp.float32) * scale
    probs = jnp.exp(scores - stat_rows[0][:, None])
    probs_low = probs.astype(jnp.bfloat16)
    prob_grad = jnp.dot(grow, val_all.T, preferred_element_type=jnp.float32)
    score_grad = (probs * (prob_grad - stat_rows[1][:, None])).astype(jnp.bfloat16)
    query_part = jnp.dot(score_grad, key_all, preferred_element_type=jnp.float32) * scale
    key_part = jnp.dot(score_grad.T, qrow, preferred_element_type=jnp.float32) * scale
    val_part = jnp.dot(probs_low.T, grow, preferred_element_type=jnp.float32)
    return (query_part, key_part, val_part)


def make_folder(stats_all, key_all, val_all, scale):

    def fold(carry, piece, start):
        qpiece, gpiece = piece
        count = qpiece.shape[0]
        width = 512

        def one(index, acc):
            query_all, key_acc, val_acc = acc
            offset = (index * width).astype(jnp.int32)
            qrow = lax.dynamic_slice_in_dim(qpiece, offset, width, 0)
            grow = lax.dynamic_slice_in_dim(gpiece, offset, width, 0)
            stat_rows = lax.dynamic_slice_in_dim(stats_all, offset, width, 1)
            query_part, key_part, val_part = tile_grads(
                qrow, grow, stat_rows, key_all, val_all, scale
            )
            query_all = lax.dynamic_update_slice_in_dim(query_all, query_part, offset, 0)
            return (query_all, key_acc + key_part, val_acc + val_part)

        return lax.fori_loop(0, count // width, one, carry)

    return fold


def starting(query_count, key_count, head):
    return (
        jnp.zeros((query_count, head), jnp.float32),
        jnp.zeros((key_count, head), jnp.float32),
        jnp.zeros((key_count, head), jnp.float32),
    )


def shards(queries, keys, values, attended, out_grad, logsumexp):
    head = queries.shape[1]
    local_rows = queries.shape[0]
    scale = head ** (-0.5)
    delta = jnp.sum(out_grad.astype(jnp.float32) * attended.astype(jnp.float32), axis=1)
    stats = jnp.stack([logsumexp, delta], 0)
    stats_all = lax.all_gather(stats, "inner", axis=1, tiled=True)
    key_all, val_all = (
        lax.all_gather(keys, "outer", axis=0, tiled=True),
        lax.all_gather(values, "outer", axis=0, tiled=True),
    )
    fold = make_folder(stats_all, key_all, val_all, scale)
    init = starting(local_rows * lax.axis_size("inner"), key_all.shape[0], head)
    query_all, key_acc, val_acc = fold(
        init,
        (
            lax.all_gather(queries, "inner", axis=0, tiled=True),
            lax.all_gather(out_grad, "inner", axis=0, tiled=True),
        ),
        jnp.int32(0),
    )
    query_grad = lax.psum_scatter(query_all, "inner", scatter_dimension=0, tiled=True)
    key_grad, value_grad = (
        lax.psum_scatter(key_acc, "outer", scatter_dimension=0, tiled=True),
        lax.psum_scatter(val_acc, "outer", scatter_dimension=0, tiled=True),
    )
    return (
        query_grad.astype(jnp.bfloat16),
        key_grad.astype(jnp.bfloat16),
        value_grad.astype(jnp.bfloat16),
    )


def solution(mesh):
    return jax.shard_map(
        shards,
        mesh=mesh,
        in_specs=(
            P(("outer", "inner"), None),
            P(("outer", "inner"), None),
            P(("outer", "inner"), None),
            P(("outer", "inner"), None),
            P(("outer", "inner"), None),
            P(("outer", "inner")),
        ),
        out_specs=(
            P(("outer", "inner"), None),
            P(("outer", "inner"), None),
            P(("outer", "inner"), None),
        ),
        check_vma=False,
    )
```

profile of v0, /device:TPU:1, one launch (start us, length us, event | category | flops | bytes accessed | tf_op | source)
XLA Modules:
  0.0 579.6 jit_solution(9206327918127201640)
XLA Ops:
  10.3 59.2 %all_gather.17 = f32[2,4096]{1,0:T(2,128)S(1)} all-gather(f32[2,128]{1,0:T(2,128)S(1)} %pad_maximum_fusion), channel_id=1, replica_groups=mesh['outer'=16,'inner'=32] {'inner'}, dimensions={1}, use_global_device_ids=true | all-gather | bytes 33792 | tf_op jit(solution)/shard_map/all_gather | solution.py:57
  69.5 38.6 %all_gather.16 = bf16[2048,128]{1,0:T(8,128)(2,1)S(1)} all-gather(bf16[128,128]{1,0:T(8,128)(2,1)} %param.9), channel_id=1, replica_groups=mesh['outer'=16,'inner'=32] {'outer'}, dimensions={0}, use_global_device_ids=true | all-gather | bytes 557056 | tf_op jit(solution)/shard_map/all_gather | solution.py:59
  108.1 34.0 %all_gather.19 = bf16[2048,128]{1,0:T(8,128)(2,1)S(1)} all-gather(bf16[128,128]{1,0:T(8,128)(2,1)} %param.10), channel_id=1, replica_groups=mesh['outer'=16,'inner'=32] {'outer'}, dimensions={0}, use_global_device_ids=true | all-gather | bytes 557056 | tf_op jit(solution)/shard_map/all_gather | solution.py:60
  142.1 49.8 %all-gather.5.cloned.1.call-done = bf16[4096,128]{1,0:T(8,128)(2,1)} async-done(((bf16[128,128]{1,0:T(8,128)(2,1)}), bf16[4096,128]{1,0:T(8,128)(2,1)}) %all-gather.5.cloned.1.call-update) | async-done | bytes 1048592 | tf_op jit(solution)/shard_map/all_gather | solution.py:68
  193.5 76.2 %while.18 = (s32[]{:T(128)}, f32[4096,128]{1,0:T(8,128)}, f32[2048,128]{1,0:T(8,128)S(1)}, f32[2048,128]{1,0:T(8,128)S(1)}, bf16[4096,128]{1,0:T(8,128)(2,1)}, /...) while((s32[]{:T(128)}, f32[4096,128]{1,0:T(8,128)}, ...), condition=%wide.region_2.0_spmd.clone, body=%wide.region_1.0_spmd.clone.sunk | while | flops 1351942144 | bytes 25442540 | solution.py:38
  195.1 2.3 convolution_add_fusion.2
  199.5 2.1 fusion.46
  204.7 2.3 convolution_add_fusion.2
  209.0 2.1 fusion.46
  214.2 2.3 convolution_add_fusion.2
  218.6 2.1 fusion.46
  223.7 2.3 convolution_add_fusion.2
  228.1 2.1 fusion.46
  233.2 2.3 convolution_add_fusion.2
  237.6 2.1 fusion.46
  242.8 2.3 convolution_add_fusion.2
  247.1 2.1 fusion.46
  252.3 2.3 convolution_add_fusion.2
  256.6 2.1 fusion.46
  261.8 2.3 convolution_add_fusion.2
  266.2 2.1 fusion.46
  271.8 69.4 %reduce-scatter.8.cloned.1.call-done = f32[128,128]{1,0:T(8,128)} async-done(((f32[2048,128]{1,0:T(8,128)}), f32[128,128]{1,0:T(8,128)}) %reduce-scatter.8.cloned.1.call-update) | async-done | bytes 65552 | tf_op jit(solution)/shard_map/reduce_scatter | solution.py:75
  342.7 85.8 %reduce-scatter.6.cloned.1.call-done = f32[128,128]{1,0:T(8,128)} async-done(((f32[2048,128]{1,0:T(8,128)}), f32[128,128]{1,0:T(8,128)}) %reduce-scatter.6.cloned.1.call-update) | async-done | bytes 65552 | tf_op jit(solution)/shard_map/reduce_scatter | solution.py:74
  430.0 141.7 %reduce-scatter.4.cloned.1.call-done = f32[128,128]{1,0:T(8,128)} async-done(((f32[4096,128]{1,0:T(8,128)}), f32[128,128]{1,0:T(8,128)}) %reduce-scatter.4.cloned.1.call-update) | async-done | bytes 65552 | tf_op jit(solution)/shard_map/reduce_scatter | solution.py:72
  (55 shorter events, 52.0 us)
Async XLA Ops:
  7.2 135.0 %all-gather.3.cloned.1.call-start = ((), (), s32[]{:S(2)}) async-start(), calls=%async_computation.3 | async-start | bytes 1081344 | tf_op jit(solution)/shard_map/all_gather | solution.py:67
  7.9 184.1 %all-gather.5.cloned.1.call-start = ((), (), s32[]{:S(2)}) async-start(), calls=%async_computation.4 | async-start | bytes 1081344 | tf_op jit(solution)/shard_map/all_gather | solution.py:68
  8.6 332.6 %reduce-scatter.8.cloned.1.call-start = ((), (), s32[]{:S(2)}) async-start(), calls=%async_computation.7 | async-start | bytes 1114112 | tf_op jit(solution)/shard_map/reduce_scatter | solution.py:75
  269.6 1.0 copy-start
  269.6 1.3 copy-start.1
  270.6 157.8 %reduce-scatter.6.cloned.1.call-start = ((), (), s32[]{:S(2)}) async-start(), calls=%async_computation.6 | async-start | bytes 1114112 | tf_op jit(solution)/shard_map/reduce_scatter | solution.py:74
  271.2 300.4 %reduce-scatter.4.cloned.1.call-start = ((), (), s32[]{:S(2)}) async-start(), calls=%async_computation.5 | async-start | bytes 2162688 | tf_op jit(solution)/shard_map/reduce_scatter | solution.py:72
Sparse Core Ops, SparseCore 0:
  11.3 92.9 all-gather.2
  107.6 84.3 all-gather.4
  270.8 70.4 reduce-scatter.7
  344.1 84.3 reduce-scatter.5
  433.0 138.5 reduce-scatter.3
where the time goes:
time: 585 us; the launch traced here: 580 us
  waiting for transfers between devices  349 us (60%)
  blocking collectives  132 us (23%)
  matrix products  75.3 us (13%)
  between operations  13.8 us (2%)
  other arithmetic  5.92 us (1%)
    reduce_scatter x1, waiting for transfers between devices, shards(): lax.psum_scatter(query_all, 'inner', scatter_dimension=0, tiled=True)  142 us
    reduce_scatter x1, waiting for transfers between devices, shards(): lax.psum_scatter(key_acc, 'outer', scatter_dimension=0, tiled=True)  85.8 us
    reduce_scatter x1, waiting for transfers between devices, shards(): lax.psum_scatter(val_acc, 'outer', scatter_dimension=0, tiled=True)  69.4 us
    all_gather x1, blocking collectives, shards(): stats_all = lax.all_gather(stats, 'inner', axis=1, tiled=True)  59.2 us
    all_gather x1, waiting for transfers between devices, shards(): lax.all_gather(out_grad, 'inner', axis=0, tiled=True)  49.8 us
    all_gather x1, blocking collectives, shards(): lax.all_gather(keys, 'outer', axis=0, tiled=True)  38.6 us
    all_gather x1, blocking collectives, shards(): lax.all_gather(values, 'outer', axis=0, tiled=True)  34 us
    dot_general x8, matrix products, tile_grads(): val_part = jnp.dot(probs_low.T, grow, preferred_element_type=jnp.float32)  18.6 us
  transfers between devices with their start and end apart: 5, of which 4 were waited for; matrix products, arithmetic and copies ran while one was open for 1% of the time, Pallas kernels for 0%

commit v1 on v0

v1 whole, which is shorter than its diff:
```python
import jax
import jax.numpy as jnp
from jax import lax
from jax.experimental import pallas as pl
from jax.experimental.pallas import tpu as pltpu
from jax.sharding import PartitionSpec as P

MESH = pl.DeviceIdType.MESH
F32, BF16 = jnp.float32, jnp.bfloat16
H = 128
QP, KP = 2 * H, 4 * H
LOG2E = 1.4426950408889634


def dot(a, b, over_a, over_b):
    return lax.dot_general(
        a, b, (((over_a,), (over_b,)), ((), ())), preferred_element_type=F32
    )


def thirds(row):
    high = row.astype(BF16).astype(F32)
    rest = row - high
    middle = rest.astype(BF16).astype(F32)
    return high, middle, rest - middle


def kernel(
    q_ref, k_ref, v_ref, a_ref, g_ref, l_ref,
    oq_ref, ok_ref, ov_ref,
    qg, qs, kg, dq, dk, dv, pb, db,
    q_out, q_in, q_mine, q_theirs,
    c_out, c_in, k_out, k_in, k_mine, k_theirs,
    send, recv,
):
    scale = H ** (-0.5)
    outer, inner = lax.axis_index("outer"), lax.axis_index("inner")
    x, z_lo = outer % 4, outer // 4
    y, z_hi, core = inner // 4, (inner // 2) % 2, inner % 2
    z = z_hi * 4 + z_lo

    def device(x, y, z, core):
        return ((z % 4) * 4 + x, y * 4 + (z // 4) * 2 + core)

    sibling = device(x, y, z, 1 - core)
    q_pair = device(x + 1 - 2 * (x % 2), y, z, core)
    k_pair = device(3 - x, y, z, core)
    z_ring = (device(x, y, (z + 1) % 8, core), device(x, y, (z + 7) % 8, core))
    y_ring = (device(x, (y + 1) % 8, z, core), device(x, (y + 7) % 8, z, core))

    barrier = pltpu.get_barrier_semaphore()
    for other in (sibling, q_pair, k_pair, *z_ring, *y_ring):
        pl.semaphore_signal(barrier, inc=1, device_id=other, device_id_type=MESH)

    copies = {}

    def start(name, src, dst, to):
        index = len(copies)
        copies[name] = pltpu.make_async_remote_copy(
            src_ref=src, dst_ref=dst, send_sem=send.at[index], recv_sem=recv.at[index],
            device_id=to, device_id_type=MESH,
        )
        copies[name].start()

    def arrived(*names):
        for name in names:
            copies[name].wait_recv()

    main = pl.ds(H, 2 * H)
    qg[0:H, H : 2 * H] = q_ref[...]
    qg[0:H, 2 * H : 3 * H] = g_ref[...]
    kg[0:H, H : 2 * H] = k_ref[...]
    kg[0:H, 2 * H : 3 * H] = v_ref[...]
    product = g_ref[...].astype(F32) * a_ref[...].astype(F32)
    delta = jnp.sum(product.T, axis=0, keepdims=True)
    line = lax.broadcasted_iota(jnp.int32, (16, H), 0)
    stats = jnp.zeros((16, H), F32)
    for at, row in enumerate((*thirds(l_ref[...] * (H**0.5)), *thirds(delta))):
        stats = jnp.where(line == at, row, stats)
    qs[0] = stats.astype(BF16)

    pl.semaphore_wait(barrier, 7)

    def send_queries(name, src, dst, block, count, to):
        rows = lambda slot: pl.ds(slot * QP + block * H, count * H)
        some = lambda slot: pl.ds(slot * 2 + block, count)
        start(name, qg.at[rows(src), main], qg.at[rows(dst), main], to)
        start(name + "s", qs.at[some(src)], qs.at[some(dst)], to)

    def send_keys(name, src, dst, block, count, to):
        rows = lambda slot: pl.ds(slot * KP + block * H, count * H)
        start(name, kg.at[rows(src), main], kg.at[rows(dst), main], to)

    def share_keys(name, slot, block, count):
        here = pl.ds(slot * KP + block * H, count * H)
        there = pl.ds(slot * KP + (2 + block) * H, count * H)
        start(name, kg.at[here, main], kg.at[there, main], sibling)

    here, there = pl.ds(0, H), pl.ds(H, H)
    start("qx", qg.at[here, main], qg.at[there, main], q_pair)
    start("qxs", qs.at[pl.ds(0, 1)], qs.at[pl.ds(1, 1)], q_pair)
    start("kx", kg.at[here, main], kg.at[there, main], k_pair)
    for way in range(2):
        send_queries(f"q1{way}a", 0, 1 + way, 0, 1, z_ring[way])
        send_keys(f"k1{way}a", 0, 1 + way, 0, 1, y_ring[way])
    share_keys("c0a", 0, 0, 1)

    lane = lax.broadcasted_iota(jnp.int32, (KP, H), 1)
    minus = jnp.where(lane < 3, -1.0, 0.0).astype(BF16)

    def clear(slot, _):
        rows = pl.ds(pl.multiple_of(slot * KP, KP), KP)
        kg[rows, 0:H] = minus
        kg[rows, 3 * H : 4 * H] = minus
        dk[:, rows] = jnp.zeros((H, KP), F32)
        dv[:, rows] = jnp.zeros((H, KP), F32)
        some = pl.ds(pl.multiple_of(slot * QP, QP), QP)
        dq[some, :] = jnp.zeros((QP, H), F32)

    lax.fori_loop(0, 8, clear, None)

    spread_at = lax.broadcasted_iota(jnp.int32, (16, H), 1)
    spread_l = jnp.where((line == spread_at) & (line < 3), 1.0, 0.0).astype(BF16)
    spread_d = jnp.where((line == spread_at + 3) & (line < 6), 1.0, 0.0).astype(BF16)

    def prepare(slot):
        for block in range(2):
            rows = pl.ds(slot * QP + block * H, H)
            these = qs[slot * 2 + block]
            qg[rows, 0:H] = dot(these, spread_l, 0, 0).astype(BF16)
            qg[rows, 3 * H : 4 * H] = dot(these, spread_d, 0, 0).astype(BF16)

    def tiles(first, count, columns):
        at, size = first * QP, count * QP
        rows = pl.ds(at, size)

        def one(slot):
            keys = pl.ds(pl.multiple_of(slot * KP, KP), KP)
            probs = jnp.exp2(dot(qg[rows, 0 : 2 * H], kg[keys, 0 : 2 * H], 1, 1) * (scale * LOG2E))
            shifted = dot(qg[rows, 2 * H : 4 * H], kg[keys, 2 * H : 4 * H], 1, 1)
            db[0:size] = (probs * shifted).astype(BF16)
            pb[0:size] = probs.astype(BF16)
            dv[:, keys] += dot(qg[rows, 2 * H : 3 * H], pb[0:size], 0, 0)
            dk[:, keys] += dot(qg[rows, H : 2 * H], db[0:size], 0, 0)
            dq[rows, :] += dot(db[0:size], kg[keys, H : 2 * H], 1, 0)

        low, high = columns
        if high - low == 1:
            one(low)
        else:
            lax.fori_loop(low, high, lambda slot, _: one(slot), None)

    arrived("qx", "qxs", "kx")
    for way in range(2):
        send_queries(f"q1{way}b", 0, 1 + way, 1, 1, z_ring[way])
        send_keys(f"k1{way}b", 0, 1 + way, 1, 1, y_ring[way])
    share_keys("c0b", 0, 1, 1)
    prepare(0)
    for way in range(2):
        arrived(f"q1{way}a", f"q1{way}as", f"q1{way}b", f"q1{way}bs")
        send_queries(f"q2{way}", 1 + way, 3 + way, 0, 2, z_ring[way])
        arrived(f"k1{way}a", f"k1{way}b")
        send_keys(f"k2{way}", 1 + way, 3 + way, 0, 2, y_ring[way])
        share_keys(f"c{1 + way}", 1 + way, 0, 2)
        prepare(1 + way)
    arrived("c0a", "c0b", "c1", "c2")
    tiles(0, 3, (0, 3))
    for way in range(2):
        arrived(f"q2{way}", f"q2{way}s")
        send_queries(f"q3{way}", 3 + way, 5 + way, 0, 2, z_ring[way])
        arrived(f"k2{way}")
        send_keys(f"k3{way}", 3 + way, 5 + way, 0, 2, y_ring[way])
        share_keys(f"c{3 + way}", 3 + way, 0, 2)
        prepare(3 + way)
    tiles(3, 2, (0, 3))
    arrived("c3", "c4")
    tiles(0, 5, (3, 4))
    for way in range(2):
        arrived(f"q3{way}", f"q3{way}s")
        send_queries(f"q4{way}", 5 + way, 7, way, 1, z_ring[way])
        arrived(f"k3{way}")
        send_keys(f"k4{way}", 5 + way, 7, way, 1, y_ring[way])
        share_keys(f"c{5 + way}", 5 + way, 0, 2)
        prepare(5 + way)
    tiles(0, 5, (4, 5))
    for way in range(2):
        arrived(f"q4{way}", f"q4{way}s", f"k4{way}")
    share_keys("c7", 7, 0, 2)
    prepare(7)

    def swap(slot):
        theirs = pl.ds(slot * KP + 2 * H, 2 * H)
        c_out[slot, 0] = dk[:, theirs].astype(BF16)
        c_out[slot, 1] = dv[:, theirs].astype(BF16)
        start(f"s{slot}", c_out.at[slot], c_in.at[slot], sibling)

    def mine(slot, which, grads, block, count):
        lanes = pl.ds(slot * KP + block * H, count * H)
        part = pl.ds(block * H, count * H)
        return grads[:, lanes] + c_in[slot, which, :, part].astype(F32)

    def pass_keys(step, way):
        slot = 10 - 2 * step - way
        if step == 1:
            part = pl.ds(way * H, H)
            for which, grads in enumerate((dk, dv)):
                k_out[way, 0, which, :, part] = mine(7, which, grads, way, 1).astype(BF16)
            start(
                f"ks1{way}", k_out.at[way, 0, :, :, part], k_in.at[way, 0, :, :, part], y_ring[way]
            )
            return
        arrived(f"ks{step - 1}{way}")
        for which, grads in enumerate((dk, dv)):
            for block in range(2):
                part = pl.ds(block * H, H)
                total = mine(slot, which, grads, block, 1)
                if step > 2 or block == way:
                    total += k_in[way, step - 2, which, :, part].astype(F32)
                k_out[way, step - 1, which, :, part] = total.astype(BF16)
        start(f"ks{step}{way}", k_out.at[way, step - 1], k_in.at[way, step - 1], y_ring[way])

    def pass_queries(step, way):
        slot = 10 - 2 * step - way
        if step == 1:
            part = pl.ds(way * H, H)
            q_out[way, 0, part] = dq[pl.ds(7 * QP + way * H, H), :].astype(BF16)
            start(f"qs1{way}", q_out.at[way, 0, part], q_in.at[way, 0, part], z_ring[way])
            return
        arrived(f"qs{step - 1}{way}")
        for block in range(2):
            part = pl.ds(block * H, H)
            total = dq[pl.ds(slot * QP + block * H, H), :]
            if step > 2 or block == way:
                total += q_in[way, step - 2, part].astype(F32)
            q_out[way, step - 1, part] = total.astype(BF16)
        start(f"qs{step}{way}", q_out.at[way, step - 1], q_in.at[way, step - 1], z_ring[way])

    arrived("c5", "c6", "c7")
    tiles(0, 8, (7, 8))
    swap(7)
    tiles(0, 8, (5, 6))
    swap(5)
    arrived("s7")
    pass_keys(1, 0)
    pass_keys(1, 1)
    tiles(0, 8, (6, 7))
    swap(6)
    tiles(5, 3, (3, 4))
    swap(3)
    arrived("s5", "s6")
    pass_keys(2, 0)
    pass_keys(2, 1)
    tiles(5, 3, (4, 5))
    swap(4)
    tiles(5, 3, (1, 3))
    swap(1)
    swap(2)
    tiles(5, 3, (0, 1))
    swap(0)
    for way in range(2):
        pass_queries(1, way)
    arrived("s3", "s4")
    for way in range(2):
        pass_keys(3, way)
    arrived("s0", "s1", "s2")
    for step in (2, 3, 4):
        for way in range(2):
            pass_queries(step, way)
        if step == 3:
            for way in range(2):
                pass_keys(4, way)

    arrived("qs40", "qs41")

    def own_queries(block):
        part = pl.ds(block * H, H)
        return dq[part, :] + q_in[0, 3, part].astype(F32) + q_in[1, 3, part].astype(F32)

    q_mine[...] = own_queries(1).astype(BF16)
    start("qp", q_mine, q_theirs, q_pair)

    def own_keys(which, grads, block):
        part = pl.ds(block * H, H)
        total = mine(0, which, grads, block, 1)
        for way in range(2):
            total += k_in[way, 3, which, :, part].astype(F32)
        return total

    arrived("ks40", "ks41")
    for which, grads in enumerate((dk, dv)):
        k_mine[which] = own_keys(which, grads, 1).astype(BF16)
    start("kp", k_mine, k_theirs, k_pair)
    arrived("qp")
    oq_ref[...] = ((own_queries(0) + q_theirs[...].astype(F32)) * scale).astype(BF16)
    arrived("kp")
    for which, (grads, out, by) in enumerate(((dk, ok_ref, scale), (dv, ov_ref, 1.0))):
        total = own_keys(which, grads, 0) + k_theirs[which].astype(F32)
        out[...] = (total * by).T.astype(BF16)
    for copy in copies.values():
        copy.wait_send()


COPIES = 96


def shards(queries, keys, values, attended, out_grad, logsumexp):
    vmem = pl.BlockSpec(memory_space=pltpu.VMEM)
    block = jax.ShapeDtypeStruct((H, H), BF16)
    return pl.pallas_call(
        kernel,
        out_shape=(block, block, block),
        in_specs=[vmem] * 6,
        out_specs=[vmem] * 3,
        scratch_shapes=[
            pltpu.VMEM((8 * QP, 4 * H), BF16),
            pltpu.VMEM((16, 16, H), BF16),
            pltpu.VMEM((8 * KP, 4 * H), BF16),
            pltpu.VMEM((8 * QP, H), F32),
            pltpu.VMEM((H, 8 * KP), F32),
            pltpu.VMEM((H, 8 * KP), F32),
            pltpu.VMEM((8 * QP, KP), BF16),
            pltpu.VMEM((8 * QP, KP), BF16),
            pltpu.VMEM((2, 4, QP, H), BF16),
            pltpu.VMEM((2, 4, QP, H), BF16),
            pltpu.VMEM((H, H), BF16),
            pltpu.VMEM((H, H), BF16),
            pltpu.VMEM((8, 2, H, 2 * H), BF16),
            pltpu.VMEM((8, 2, H, 2 * H), BF16),
            pltpu.VMEM((2, 4, 2, H, 2 * H), BF16),
            pltpu.VMEM((2, 4, 2, H, 2 * H), BF16),
            pltpu.VMEM((2, H, H), BF16),
            pltpu.VMEM((2, H, H), BF16),
            pltpu.SemaphoreType.DMA((COPIES,)),
            pltpu.SemaphoreType.DMA((COPIES,)),
        ],
        compiler_params=pltpu.CompilerParams(
            collective_id=0, has_side_effects=True, vmem_limit_bytes=56 * 2**20
        ),
    )(queries, keys, values, attended, out_grad, logsumexp.reshape(1, H))


def solution(mesh):
    rows, flat = P(("outer", "inner"), None), P(("outer", "inner"))
    return jax.shard_map(
        shards,
        mesh=mesh,
        in_specs=(rows, rows, rows, rows, rows, flat),
        out_specs=(rows, rows, rows),
        check_vma=False,
    )
```

time: 585 us -> 74.8 us (0.13)
  the two profiles are of different devices: /device:TPU:1 before, /device:TPU:64 now
where the time goes in v1:
time: 74.8 us; the launch traced here: 74.5 us
  Pallas kernels  71.1 us (95%)
  local copies, waits for them, and re-layouts  2.77 us (4%)
    pallas_call x1, Pallas kernels, shards(): pl.pallas_call(kernel, out_shape=(block, block, block), in_specs=[vmem] *...  71.1 us
    unnamed x7, local copies, waits for them, and re-layouts  2.77 us

profile of v1, /device:TPU:64, one launch (start us, length us, event | category | flops | bytes accessed | tf_op | source)
XLA Modules:
  0.0 74.5 jit_solution(29132319244320304)
XLA Ops:
  0.6 71.1 %shard_map.85 = (bf16[128,128]{1,0:T(8,128)(2,1)}, bf16[128,128]{1,0:T(8,128)(2,1)}, bf16[128,128]{1,0:T(8,128)(2,1)}) custom-call(bf16[128,128]{1,0:T(8,128)(2,1)} %q_ref.1, bf16[128,128]{1,0:T(8,128)(2,1)} %k_ref.1, bf16[128,128]{1,0:T(8,128)(2,1)} %v_ref.1, bf16[128,128]{1,0:T(8,128)(2,1)} %a_ref.1, bf16[128,128]{1,0:T(8,128)(2,1)} %g_ref.1, f32[1,128]{1,0:T(1,128)} %bitcast.1), custom_call_target="tpu_custom_call" | custom-call | tf_op jit(solution)/shard_map/pallas_call | solution.py:309
  71.7 0.0 copy-start.1
  71.7 1.4 %copy.12 = bf16[128,128]{1,0:T(8,128)(2,1)} copy(bf16[128,128]{1,0:T(8,128)(2,1)} %get-tuple-element.6) | data formatting | bytes 65536
  73.1 0.0 copy-done.1
  73.1 0.0 copy-start
  73.1 0.6 copy.13
  73.7 0.2 copy-done
  73.9 0.6 copy.14
Async XLA Ops:
  71.7 1.4 %copy-start.1 = (bf16[128,128]{1,0:T(8,128)(2,1)S(1)}, bf16[128,128]{1,0:T(8,128)(2,1)}, u32[]{:S(2)}) copy-start(bf16[128,128]{1,0:T(8,128)(2,1)} %get-tuple-element.7) | copy-start | bytes 98308
  73.1 0.8 %copy-start = (bf16[128,128]{1,0:T(8,128)(2,1)S(1)}, bf16[128,128]{1,0:T(8,128)(2,1)}, u32[]{:S(2)}) copy-start(bf16[128,128]{1,0:T(8,128)(2,1)} %get-tuple-element.8) | copy-start | bytes 98308

commit v2 on v0

v2 whole, which is shorter than its diff:
```python
import jax
import jax.numpy as jnp
from jax import lax
from jax.experimental import pallas as pl
from jax.experimental.pallas import tpu as pltpu
from jax.sharding import PartitionSpec as P

MESH = pl.DeviceIdType.MESH
F32, BF16 = jnp.float32, jnp.bfloat16
H = 128
LEVEL = 4 * H
OFFSETS = (0, -1, 1, -2, 2, -3, 3, 4)
OWN = (0, 2, 3, 4, 5, 8, 9, 12)
PAIR = (1, 6, 7, 10, 11, 13, 14, 15)
LOG2E = 1.4426950408889634


def dot(a, b, over_a, over_b):
    return lax.dot_general(
        a, b, (((over_a,), (over_b,)), ((), ())), preferred_element_type=F32
    )


def thirds(row):
    high = row.astype(BF16).astype(F32)
    rest = row - high
    middle = rest.astype(BF16).astype(F32)
    return high, middle, rest - middle


def kernel(
    q_ref, k_ref, v_ref, a_ref, g_ref, l_ref,
    oq_ref, ok_ref, ov_ref,
    qg, qs, kg, dq, dk, dv, pb, db,
    c_out, c_in, kx_out, kx_in, k_out, k_in, qx_out, qx_in, q_out, q_in,
    send, recv,
):
    scale = H ** (-0.5)
    outer, inner = lax.axis_index("outer"), lax.axis_index("inner")
    x, z_lo = outer % 4, outer // 4
    y, z_hi, core = inner // 4, (inner // 2) % 2, inner % 2
    z = z_hi * 4 + z_lo

    def device(x, y, z, core):
        return ((z % 4) * 4 + x, y * 4 + (z // 4) * 2 + core)

    sibling = device(x, y, z, 1 - core)
    q_pair = device(x + 1 - 2 * (x % 2), y, z, core)
    k_pair = device(3 - x, y, z, core)

    def z_ring(offset):
        return device(x, y, (z + offset + 8) % 8, core)

    def y_ring(offset):
        return device(x, (y + offset + 8) % 8, z, core)

    barrier = pltpu.get_barrier_semaphore()
    others = [sibling, q_pair, k_pair]
    for offset in OFFSETS[1:]:
        others += [z_ring(offset), y_ring(offset)]
    for other in others:
        pl.semaphore_signal(barrier, inc=1, device_id=other, device_id_type=MESH)

    copies = {}

    def start(name, src, dst, to):
        index = len(copies)
        copies[name] = pltpu.make_async_remote_copy(
            src_ref=src, dst_ref=dst, send_sem=send.at[index], recv_sem=recv.at[index],
            device_id=to, device_id_type=MESH,
        )
        copies[name].start()

    def arrived(*names):
        for name in names:
            copies[name].wait_recv()

    main = pl.ds(H, 2 * H)
    qg[0:H, H : 2 * H] = q_ref[...]
    qg[0:H, 2 * H : 3 * H] = g_ref[...]
    kg[0:H, H : 2 * H] = k_ref[...]
    kg[0:H, 2 * H : 3 * H] = v_ref[...]
    product = g_ref[...].astype(F32) * a_ref[...].astype(F32)
    delta = jnp.sum(product.T, axis=0, keepdims=True)
    line = lax.broadcasted_iota(jnp.int32, (16, H), 0)
    stats = jnp.zeros((16, H), F32)
    for at, row in enumerate((*thirds(l_ref[...] * (H**0.5)), *thirds(delta))):
        stats = jnp.where(line == at, row, stats)
    qs[0] = stats.astype(BF16)

    pl.semaphore_wait(barrier, len(others))

    def key_rows(block, count):
        return pl.ds((block // 4) * 2 * LEVEL + (block % 4) * H, count * H)

    def send_queries(name, src, dst, count, to):
        start(
            name, qg.at[pl.ds(src * H, count * H), main], qg.at[pl.ds(dst * H, count * H), main], to
        )
        start(name + "s", qs.at[pl.ds(src, count)], qs.at[pl.ds(dst, count)], to)

    def send_keys(name, src, dst, count, to):
        start(name, kg.at[key_rows(src, count), main], kg.at[key_rows(dst, count), main], to)

    def share_keys(level):
        here, there = level * 2 * LEVEL, (level * 2 + 1) * LEVEL
        start(f"c{level}", kg.at[pl.ds(here, LEVEL), main], kg.at[pl.ds(there, LEVEL), main], sibling)

    def hand_on(slot, count):
        send_queries(f"qx{slot}", OWN[slot], PAIR[slot], count, q_pair)
        send_keys(f"kx{slot}", OWN[slot], PAIR[slot], count, k_pair)

    def came(*slots):
        for slot in slots:
            arrived(f"q{slot}", f"q{slot}s", f"k{slot}")

    def handed(*slots):
        for slot in slots:
            arrived(f"qx{slot}", f"qx{slot}s", f"kx{slot}")

    for slot in (1, 2):
        send_queries(f"q{slot}", 0, OWN[slot], 1, z_ring(-OFFSETS[slot]))
        send_keys(f"k{slot}", 0, OWN[slot], 1, y_ring(-OFFSETS[slot]))
    hand_on(0, 1)
    for slot in range(3, 8):
        send_queries(f"q{slot}", 0, OWN[slot], 1, z_ring(-OFFSETS[slot]))
        send_keys(f"k{slot}", 0, OWN[slot], 1, y_ring(-OFFSETS[slot]))

    lane = lax.broadcasted_iota(jnp.int32, (LEVEL, H), 1)
    minus = jnp.where(lane < 3, -1.0, 0.0).astype(BF16)

    def clear(column, _):
        rows = pl.ds(pl.multiple_of(column * LEVEL, LEVEL), LEVEL)
        kg[rows, 0:H] = minus
        kg[rows, 3 * H : 4 * H] = minus
        dk[:, rows] = jnp.zeros((H, LEVEL), F32)
        dv[:, rows] = jnp.zeros((H, LEVEL), F32)
        some = pl.ds(pl.multiple_of(column * 2 * H, 2 * H), 2 * H)
        dq[some, :] = jnp.zeros((2 * H, H), F32)

    lax.fori_loop(0, 8, clear, None)

    spread_at = lax.broadcasted_iota(jnp.int32, (16, H), 1)
    spread_l = jnp.where((line == spread_at) & (line < 3), 1.0, 0.0).astype(BF16)
    spread_d = jnp.where((line == spread_at + 3) & (line < 6), 1.0, 0.0).astype(BF16)

    def prepare(level):
        for block in range(4 * level, 4 * level + 4):
            rows = pl.ds(block * H, H)
            these = qs[block]
            qg[rows, 0:H] = dot(these, spread_l, 0, 0).astype(BF16)
            qg[rows, 3 * H : 4 * H] = dot(these, spread_d, 0, 0).astype(BF16)

    def tiles(first, count, *columns):
        size = count * LEVEL
        rows = pl.ds(first * LEVEL, size)

        def one(column):
            keys = pl.ds(pl.multiple_of(column * LEVEL, LEVEL), LEVEL)
            probs = jnp.exp2(dot(qg[rows, 0 : 2 * H], kg[keys, 0 : 2 * H], 1, 1) * (scale * LOG2E))
            shifted = dot(qg[rows, 2 * H : 4 * H], kg[keys, 2 * H : 4 * H], 1, 1)
            db[0:size] = (probs * shifted).astype(BF16)
            pb[0:size] = probs.astype(BF16)
            dv[:, keys] += dot(qg[rows, 2 * H : 3 * H], pb[0:size], 0, 0)
            dk[:, keys] += dot(qg[rows, H : 2 * H], db[0:size], 0, 0)
            dq[rows, :] += dot(db[0:size], kg[keys, H : 2 * H], 1, 0)

        if len(columns) == 1:
            one(columns[0])
        else:
            by = columns[1] - columns[0]
            lax.fori_loop(
                0, len(columns), lambda index, _: one(columns[0] + by * index), None
            )

    came(1, 2)
    hand_on(1, 2)
    handed(0)
    share_keys(0)
    prepare(0)
    tiles(0, 1, 0)
    came(3, 4)
    hand_on(3, 2)
    arrived("c0")
    tiles(0, 1, 1)
    handed(1)
    share_keys(1)
    prepare(1)
    tiles(1, 1, 0, 1)
    came(5, 6)
    hand_on(5, 2)
    arrived("c1")
    tiles(0, 2, 2, 3)
    came(7)
    hand_on(7, 1)
    handed(3)
    share_keys(2)
    prepare(2)
    arrived("c2")
    tiles(0, 2, 4, 5)
    handed(5, 7)
    share_keys(3)
    prepare(3)
    arrived("c3")

    def swap(level):
        theirs = pl.ds((2 * level + 1) * LEVEL, LEVEL)
        c_out[level, 0] = dk[:, theirs].astype(BF16)
        c_out[level, 1] = dv[:, theirs].astype(BF16)
        start(f"s{level}", c_out.at[level], c_in.at[level], sibling)

    def key_sum(which, block, count):
        grads = (dk, dv)[which]
        level, part = block // 4, pl.ds((block % 4) * H, count * H)
        here = pl.ds(level * 2 * LEVEL + (block % 4) * H, count * H)
        return grads[:, here] + c_in[level, which, :, part].astype(F32)

    def slots(first, count):
        return pl.ds(first * H, count * H)

    def keys_to_pair(first, count):
        part = slots(first, count)
        for which in range(2):
            kx_out[which, :, part] = key_sum(which, PAIR[first], count).astype(BF16)
        start(f"dkx{first}", kx_out.at[:, :, part], kx_in.at[:, :, part], k_pair)

    def key_total(which, slot):
        return key_sum(which, OWN[slot], 1) + kx_in[which, :, slots(slot, 1)].astype(F32)

    def keys_to_owner(slot):
        for which in range(2):
            k_out[slot, which] = key_total(which, slot).astype(BF16)
        start(f"dk{slot}", k_out.at[slot], k_in.at[slot], y_ring(OFFSETS[slot]))

    def queries_to_pair(first, count):
        part = slots(first, count)
        qx_out[part] = dq[slots(PAIR[first], count), :].astype(BF16)
        start(f"dqx{first}", qx_out.at[part], qx_in.at[part], q_pair)

    def query_total(slot):
        return dq[slots(OWN[slot], 1), :] + qx_in[slots(slot, 1)].astype(F32)

    def queries_to_owner(slot):
        q_out[slot] = query_total(slot).astype(BF16)
        start(f"dq{slot}", q_out.at[slot], q_in.at[slot], z_ring(OFFSETS[slot]))

    tiles(0, 4, 7)
    swap(3)
    tiles(0, 4, 6)
    arrived("s3")
    keys_to_pair(7, 1)
    keys_to_pair(5, 2)
    tiles(2, 2, 5)
    swap(2)
    queries_to_pair(1, 2)
    queries_to_pair(0, 1)
    tiles(2, 2, 4)
    arrived("s2")
    keys_to_pair(3, 2)
    tiles(3, 1, 3, 2)
    arrived("dkx7")
    keys_to_owner(7)
    tiles(3, 1, 1, 0)
    queries_to_pair(7, 1)
    queries_to_pair(5, 2)
    arrived("dkx5")
    keys_to_owner(5)
    keys_to_owner(6)
    arrived("dqx0", "dqx1")
    queries_to_owner(1)
    queries_to_owner(2)
    tiles(2, 1, 3)
    swap(1)
    tiles(2, 1, 2)
    arrived("s1")
    keys_to_pair(1, 2)
    tiles(2, 1, 1)
    swap(0)
    arrived("dkx3")
    keys_to_owner(3)
    keys_to_owner(4)
    tiles(2, 1, 0)
    queries_to_pair(3, 2)
    arrived("dqx7")
    queries_to_owner(7)
    arrived("dqx5")
    queries_to_owner(5)
    queries_to_owner(6)
    arrived("s0")
    keys_to_pair(0, 1)
    arrived("dkx1")
    keys_to_owner(1)
    keys_to_owner(2)
    arrived("dqx3")
    queries_to_owner(3)
    queries_to_owner(4)

    total = query_total(0)
    for slot in (1, 2, 7, 5, 6, 3, 4):
        arrived(f"dq{slot}")
        total += q_in[slot].astype(F32)
    oq_ref[...] = (total * scale).astype(BF16)
    arrived("dkx0")
    for slot in (7, 5, 6, 3, 4, 1, 2):
        arrived(f"dk{slot}")
    for which, (out, by) in enumerate(((ok_ref, scale), (ov_ref, 1.0))):
        total = key_total(which, 0)
        for slot in range(1, 8):
            total += k_in[slot, which].astype(F32)
        out[...] = (total * by).T.astype(BF16)
    for copy in copies.values():
        copy.wait_send()


COPIES = 80


def shards(queries, keys, values, attended, out_grad, logsumexp):
    vmem = pl.BlockSpec(memory_space=pltpu.VMEM)
    block = jax.ShapeDtypeStruct((H, H), BF16)
    keys_shape = pltpu.VMEM((2, H, 8 * H), BF16)
    return pl.pallas_call(
        kernel,
        out_shape=(block, block, block),
        in_specs=[vmem] * 6,
        out_specs=[vmem] * 3,
        scratch_shapes=[
            pltpu.VMEM((4 * LEVEL, 4 * H), BF16),
            pltpu.VMEM((16, 16, H), BF16),
            pltpu.VMEM((8 * LEVEL, 4 * H), BF16),
            pltpu.VMEM((4 * LEVEL, H), F32),
            pltpu.VMEM((H, 8 * LEVEL), F32),
            pltpu.VMEM((H, 8 * LEVEL), F32),
            pltpu.VMEM((4 * LEVEL, LEVEL), BF16),
            pltpu.VMEM((4 * LEVEL, LEVEL), BF16),
            pltpu.VMEM((4, 2, H, LEVEL), BF16),
            pltpu.VMEM((4, 2, H, LEVEL), BF16),
            keys_shape,
            keys_shape,
            pltpu.VMEM((8, 2, H, H), BF16),
            pltpu.VMEM((8, 2, H, H), BF16),
            pltpu.VMEM((8 * H, H), BF16),
            pltpu.VMEM((8 * H, H), BF16),
            pltpu.VMEM((8, H, H), BF16),
            pltpu.VMEM((8, H, H), BF16),
            pltpu.SemaphoreType.DMA((COPIES,)),
            pltpu.SemaphoreType.DMA((COPIES,)),
        ],
        compiler_params=pltpu.CompilerParams(
            collective_id=0, has_side_effects=True, vmem_limit_bytes=56 * 2**20
        ),
    )(queries, keys, values, attended, out_grad, logsumexp.reshape(1, H))


def solution(mesh):
    rows, flat = P(("outer", "inner"), None), P(("outer", "inner"))
    return jax.shard_map(
        shards,
        mesh=mesh,
        in_specs=(rows, rows, rows, rows, rows, flat),
        out_specs=(rows, rows, rows),
        check_vma=False,
    )
```

time: 585 us -> 68.3 us (0.12)
  waiting for transfers between devices: 349 us -> 0 us
  blocking collectives: 132 us -> 0 us
  matrix products: 75.3 us -> 0 us
  Pallas kernels: 0 us -> 64.6 us
  between operations: 13.8 us -> 0.65 us
  other arithmetic: 5.92 us -> 0 us
    reduce_scatter x3 -> x0, waiting for transfers between devices: 297 us -> none  [the longest x1 142 us: shards(): lax.psum_scatter(query_all, 'inner', scatter_dimension=0, tiled=True)]
    all_gather x3 -> x0, blocking collectives: 132 us -> none  [the longest x1 59.2 us: shards(): stats_all = lax.all_gather(stats, 'inner', axis=1, tiled=True)]
    dot_general x40 -> x0, matrix products: 75.3 us -> none  [the longest x8 18.6 us: tile_grads(): val_part = jnp.dot(probs_low.T, grow, preferred_element_type=jnp.float32)]
    pallas_call x0 -> x1, Pallas kernels: none -> 64.6 us  [shards(): pl.pallas_call(kernel, out_shape=(block, block, block), in_specs=[vmem] *...]
    all_gather x2 -> x0, waiting for transfers between devices: 49.8 us -> none  [the longest x1 49.8 us: shards(): lax.all_gather(out_grad, 'inner', axis=0, tiled=True)]
  transfers between devices with their start and end apart: 5 -> 0, of which waited for: 4 -> 0; matrix products, arithmetic and copies ran while one was open for 1% -> 0% of each run, Pallas kernels for 0% -> 0%
where the time goes in v2:
time: 68.3 us; the launch traced here: 68 us
  Pallas kernels  64.6 us (95%)
  local copies, waits for them, and re-layouts  2.77 us (4%)
    pallas_call x1, Pallas kernels, shards(): pl.pallas_call(kernel, out_shape=(block, block, block), in_specs=[vmem] *...  64.6 us
    unnamed x7, local copies, waits for them, and re-layouts  2.77 us

profile of v2, /device:TPU:1, one launch (start us, length us, event | category | flops | bytes accessed | tf_op | source)
XLA Modules:
  0.0 68.0 jit_solution(6776420898246618609)
XLA Ops:
  0.6 64.6 %shard_map.85 = (bf16[128,128]{1,0:T(8,128)(2,1)}, bf16[128,128]{1,0:T(8,128)(2,1)}, bf16[128,128]{1,0:T(8,128)(2,1)}) custom-call(bf16[128,128]{1,0:T(8,128)(2,1)} %q_ref.1, bf16[128,128]{1,0:T(8,128)(2,1)} %k_ref.1, bf16[128,128]{1,0:T(8,128)(2,1)} %v_ref.1, bf16[128,128]{1,0:T(8,128)(2,1)} %a_ref.1, bf16[128,128]{1,0:T(8,128)(2,1)} %g_ref.1, f32[1,128]{1,0:T(1,128)} %bitcast.1), custom_call_target="tpu_custom_call" | custom-call | tf_op jit(solution)/shard_map/pallas_call | solution.py:322
  65.2 0.0 copy-start.1
  65.2 1.4 %copy.12 = bf16[128,128]{1,0:T(8,128)(2,1)} copy(bf16[128,128]{1,0:T(8,128)(2,1)} %get-tuple-element.6) | data formatting | bytes 65536
  66.6 0.0 copy-done.1
  66.6 0.0 copy-start
  66.6 0.6 copy.13
  67.2 0.2 copy-done
  67.4 0.6 copy.14
Async XLA Ops:
  65.2 1.4 %copy-start.1 = (bf16[128,128]{1,0:T(8,128)(2,1)S(1)}, bf16[128,128]{1,0:T(8,128)(2,1)}, u32[]{:S(2)}) copy-start(bf16[128,128]{1,0:T(8,128)(2,1)} %get-tuple-element.7) | copy-start | bytes 98308
  66.6 0.8 %copy-start = (bf16[128,128]{1,0:T(8,128)(2,1)S(1)}, bf16[128,128]{1,0:T(8,128)(2,1)}, u32[]{:S(2)}) copy-start(bf16[128,128]{1,0:T(8,128)(2,1)} %get-tuple-element.8) | copy-start | bytes 98308

commit v3 on v2

--- a/solution.py
+++ b/solution.py
@@ -56,8 +56,8 @@
 
     barrier = pltpu.get_barrier_semaphore()
     others = [sibling, q_pair, k_pair]
-    for offset in OFFSETS[1:]:
-        others += [z_ring(offset), y_ring(offset)]
+    others += [z_ring(offset) for offset in OFFSETS[1:]]
+    others += [y_ring(offset) for offset in OFFSETS[1:5]]
     for other in others:
         pl.semaphore_signal(barrier, inc=1, device_id=other, device_id_type=MESH)
 
@@ -110,6 +110,18 @@
         send_queries(f"qx{slot}", OWN[slot], PAIR[slot], count, q_pair)
         send_keys(f"kx{slot}", OWN[slot], PAIR[slot], count, k_pair)
 
+    def send_on(slot, way):
+        send_queries(f"q{slot + 2}", OWN[slot], OWN[slot + 2], 1, z_ring(way))
+        send_keys(f"k{slot + 2}", OWN[slot], OWN[slot + 2], 1, y_ring(way))
+        half = H // 2
+        low = 0 if way > 0 else half
+        there = pl.ds(OWN[7] * H + low, half)
+        start(f"q7{way}", qg.at[pl.ds(OWN[slot] * H + low, half), main], qg.at[there, main], z_ring(2 * way))
+        if way > 0:
+            start("q7s", qs.at[pl.ds(OWN[slot], 1)], qs.at[pl.ds(OWN[7], 1)], z_ring(2))
+        here, there = key_rows(OWN[slot], 1).start + low, key_rows(OWN[7], 1).start + low
+        start(f"k7{way}", kg.at[pl.ds(here, half), main], kg.at[pl.ds(there, half), main], y_ring(2 * way))
+
     def came(*slots):
         for slot in slots:
             arrived(f"q{slot}", f"q{slot}s", f"k{slot}")
@@ -122,7 +134,7 @@
         send_queries(f"q{slot}", 0, OWN[slot], 1, z_ring(-OFFSETS[slot]))
         send_keys(f"k{slot}", 0, OWN[slot], 1, y_ring(-OFFSETS[slot]))
     hand_on(0, 1)
-    for slot in range(3, 8):
+    for slot in (3, 4):
         send_queries(f"q{slot}", 0, OWN[slot], 1, z_ring(-OFFSETS[slot]))
         send_keys(f"k{slot}", 0, OWN[slot], 1, y_ring(-OFFSETS[slot]))
 
@@ -180,6 +192,8 @@
     prepare(0)
     tiles(0, 1, 0)
     came(3, 4)
+    send_on(3, 1)
+    send_on(4, -1)
     hand_on(3, 2)
     arrived("c0")
     tiles(0, 1, 1)
@@ -189,18 +203,20 @@
     tiles(1, 1, 0, 1)
     came(5, 6)
     hand_on(5, 2)
-    arrived("c1")
-    tiles(0, 2, 2, 3)
-    came(7)
-    hand_on(7, 1)
     handed(3)
     share_keys(2)
     prepare(2)
+    arrived("c1")
+    tiles(0, 2, 2)
+    arrived("q71", "q7-1", "q7s", "k71", "k7-1")
+    hand_on(7, 1)
+    tiles(0, 2, 3)
     arrived("c2")
-    tiles(0, 2, 4, 5)
+    tiles(0, 3, 4, 5)
     handed(5, 7)
     share_keys(3)
     prepare(3)
+    tiles(2, 1, 0, 1, 2, 3)
     arrived("c3")
 
     def swap(level):
@@ -225,12 +241,22 @@
         start(f"dkx{first}", kx_out.at[:, :, part], kx_in.at[:, :, part], k_pair)
 
     def key_total(which, slot):
-        return key_sum(which, OWN[slot], 1) + kx_in[which, :, slots(slot, 1)].astype(F32)
+        total = key_sum(which, OWN[slot], 1) + kx_in[which, :, slots(slot, 1)].astype(F32)
+        if slot in (3, 4):
+            total += k_in[slot + 2, which].astype(F32)
+            if which == 4 - slot:
+                total += k_in[7, which].astype(F32)
+        return total
 
     def keys_to_owner(slot):
         for which in range(2):
             k_out[slot, which] = key_total(which, slot).astype(BF16)
-        start(f"dk{slot}", k_out.at[slot], k_in.at[slot], y_ring(OFFSETS[slot]))
+        if slot == 7:
+            for which, to in enumerate((2, -2)):
+                start(f"dk7{which}", k_out.at[7, which], k_in.at[7, which], y_ring(to))
+        else:
+            to = {5: -1, 6: 1}.get(slot, OFFSETS[slot])
+            start(f"dk{slot}", k_out.at[slot], k_in.at[slot], y_ring(to))
 
     def queries_to_pair(first, count):
         part = slots(first, count)
@@ -250,62 +276,56 @@
     arrived("s3")
     keys_to_pair(7, 1)
     keys_to_pair(5, 2)
-    tiles(2, 2, 5)
-    swap(2)
     queries_to_pair(1, 2)
     queries_to_pair(0, 1)
-    tiles(2, 2, 4)
+    queries_to_pair(3, 2)
+    tiles(3, 1, 5)
+    swap(2)
+    tiles(3, 1, 4)
     arrived("s2")
     keys_to_pair(3, 2)
-    tiles(3, 1, 3, 2)
+    tiles(3, 1, 3)
+    swap(1)
+    tiles(3, 1, 2)
+    arrived("s1")
+    keys_to_pair(1, 2)
     arrived("dkx7")
     keys_to_owner(7)
-    tiles(3, 1, 1, 0)
-    queries_to_pair(7, 1)
-    queries_to_pair(5, 2)
     arrived("dkx5")
     keys_to_owner(5)
     keys_to_owner(6)
-    arrived("dqx0", "dqx1")
-    queries_to_owner(1)
-    queries_to_owner(2)
-    tiles(2, 1, 3)
-    swap(1)
-    tiles(2, 1, 2)
-    arrived("s1")
-    keys_to_pair(1, 2)
-    tiles(2, 1, 1)
+    tiles(3, 1, 1)
     swap(0)
-    arrived("dkx3")
+    arrived("dqx0", "dqx1", "dqx3")
+    for slot in range(1, 5):
+        queries_to_owner(slot)
+    tiles(3, 1, 0)
+    queries_to_pair(7, 1)
+    queries_to_pair(5, 2)
+    arrived("s0")
+    keys_to_pair(0, 1)
+    arrived("dkx3", "dk70", "dk71", "dk5", "dk6")
     keys_to_owner(3)
     keys_to_owner(4)
-    tiles(2, 1, 0)
-    queries_to_pair(3, 2)
+    arrived("dkx1")
+    keys_to_owner(1)
+    keys_to_owner(2)
     arrived("dqx7")
     queries_to_owner(7)
     arrived("dqx5")
     queries_to_owner(5)
     queries_to_owner(6)
-    arrived("s0")
-    keys_to_pair(0, 1)
-    arrived("dkx1")
-    keys_to_owner(1)
-    keys_to_owner(2)
-    arrived("dqx3")
-    queries_to_owner(3)
-    queries_to_owner(4)
 
     total = query_total(0)
-    for slot in (1, 2, 7, 5, 6, 3, 4):
+    for slot in range(1, 8):
         arrived(f"dq{slot}")
         total += q_in[slot].astype(F32)
     oq_ref[...] = (total * scale).astype(BF16)
     arrived("dkx0")
-    for slot in (7, 5, 6, 3, 4, 1, 2):
-        arrived(f"dk{slot}")
+    arrived("dk3", "dk4", "dk1", "dk2")
     for which, (out, by) in enumerate(((ok_ref, scale), (ov_ref, 1.0))):
         total = key_total(which, 0)
-        for slot in range(1, 8):
+        for slot in range(1, 5):
             total += k_in[slot, which].astype(F32)
         out[...] = (total * by).T.astype(BF16)
     for copy in copies.values():

time: 68.3 us -> 64.8 us (0.949); the launches traced: 68 us -> 63.8 us
  Pallas kernels: 64.6 us -> 60.4 us
    pallas_call x1, Pallas kernels: 64.6 us -> 60.4 us  [shards(): pl.pallas_call(kernel, out_shape=(block, block, block), in_specs=[vmem] *...]
where the time goes in v3:
time: 64.8 us; the launch traced here: 63.8 us
  Pallas kernels  60.4 us (93%)
  local copies, waits for them, and re-layouts  2.77 us (4%)
  between operations  0.65 us (1%)
    pallas_call x1, Pallas kernels, shards(): pl.pallas_call(kernel, out_shape=(block, block, block), in_specs=[vmem] *...  60.4 us
    unnamed x7, local copies, waits for them, and re-layouts  2.77 us

profile of v3, /device:TPU:1, one launch (start us, length us, event | category | flops | bytes accessed | tf_op | source)
XLA Modules:
  0.0 63.8 jit_solution(17103555972480468102)
XLA Ops:
  0.6 60.4 %shard_map.85 = (bf16[128,128]{1,0:T(8,128)(2,1)}, bf16[128,128]{1,0:T(8,128)(2,1)}, bf16[128,128]{1,0:T(8,128)(2,1)}) custom-call(bf16[128,128]{1,0:T(8,128)(2,1)} %q_ref.1, bf16[128,128]{1,0:T(8,128)(2,1)} %k_ref.1, bf16[128,128]{1,0:T(8,128)(2,1)} %v_ref.1, bf16[128,128]{1,0:T(8,128)(2,1)} %a_ref.1, bf16[128,128]{1,0:T(8,128)(2,1)} %g_ref.1, f32[1,128]{1,0:T(1,128)} %bitcast.1), custom_call_target="tpu_custom_call" | custom-call | tf_op jit(solution)/shard_map/pallas_call | solution.py:342
  61.0 0.0 copy-start.1
  61.0 1.4 %copy.12 = bf16[128,128]{1,0:T(8,128)(2,1)} copy(bf16[128,128]{1,0:T(8,128)(2,1)} %get-tuple-element.6) | data formatting | bytes 65536
  62.4 0.0 copy-done.1
  62.4 0.0 copy-start
  62.4 0.6 copy.13
  63.0 0.2 copy-done
  63.2 0.6 copy.14
Async XLA Ops:
  61.0 1.4 %copy-start.1 = (bf16[128,128]{1,0:T(8,128)(2,1)S(1)}, bf16[128,128]{1,0:T(8,128)(2,1)}, u32[]{:S(2)}) copy-start(bf16[128,128]{1,0:T(8,128)(2,1)} %get-tuple-element.7) | copy-start | bytes 98308
  62.4 0.8 %copy-start = (bf16[128,128]{1,0:T(8,128)(2,1)S(1)}, bf16[128,128]{1,0:T(8,128)(2,1)}, u32[]{:S(2)}) copy-start(bf16[128,128]{1,0:T(8,128)(2,1)} %get-tuple-element.8) | copy-start | bytes 98308

commit v4 on v2

v4 whole, which is shorter than its diff:
```python
import jax
import jax.numpy as jnp
from jax import lax
from jax.experimental import pallas as pl
from jax.experimental.pallas import tpu as pltpu
from jax.sharding import PartitionSpec as P

MESH = pl.DeviceIdType.MESH
F32, BF16 = jnp.float32, jnp.bfloat16
H = 128
LEVEL = 4 * H
OFFSETS = (0, -1, 1, -2, 2, -3, 3, 4)
OWN = (0, 2, 3, 4, 5, 8, 9, 12)
PAIR = (1, 6, 7, 10, 11, 13, 14, 15)
LOG2E = 1.4426950408889634


def dot(a, b, over_a, over_b):
    return lax.dot_general(
        a, b, (((over_a,), (over_b,)), ((), ())), preferred_element_type=F32
    )


def thirds(row):
    high = row.astype(BF16).astype(F32)
    rest = row - high
    middle = rest.astype(BF16).astype(F32)
    return high, middle, rest - middle


def kernel(
    q_ref, k_ref, v_ref, a_ref, g_ref, l_ref,
    out_ref,
    own_a, own_l, load, pw, dw,
    qg, qs, kg, dq, dk, dv, pb, db,
    c_out, c_in, kx_out, kx_in, k_out, k_in, qx_out, qx_in, q_out, q_in,
    send, recv,
):
    scale = H ** (-0.5)
    outer, inner = lax.axis_index("outer"), lax.axis_index("inner")
    x, z_lo = outer % 4, outer // 4
    y, z_hi, core = inner // 4, (inner // 2) % 2, inner % 2
    z = z_hi * 4 + z_lo

    def device(x, y, z, core):
        return ((z % 4) * 4 + x, y * 4 + (z // 4) * 2 + core)

    sibling = device(x, y, z, 1 - core)
    q_pair = device(x + 1 - 2 * (x % 2), y, z, core)
    k_pair = device(3 - x, y, z, core)

    def z_ring(offset):
        return device(x, y, (z + offset + 8) % 8, core)

    def y_ring(offset):
        return device(x, (y + offset + 8) % 8, z, core)

    barrier = pltpu.get_barrier_semaphore()
    others = [sibling, q_pair, k_pair]
    others += [z_ring(offset) for offset in OFFSETS[1:]]
    others += [y_ring(offset) for offset in OFFSETS[1:7]]
    for other in others:
        pl.semaphore_signal(barrier, inc=1, device_id=other, device_id_type=MESH)

    copies = {}

    def start(name, src, dst, to):
        index = len(copies)
        copies[name] = pltpu.make_async_remote_copy(
            src_ref=src, dst_ref=dst, send_sem=send.at[index], recv_sem=recv.at[index],
            device_id=to, device_id_type=MESH,
        )
        copies[name].start()

    def arrived(*names):
        for name in names:
            copies[name].wait_recv()

    main = pl.ds(H, 2 * H)
    mine, low, high = pl.ds(0, H), pl.ds(H, H), pl.ds(2 * H, H)
    loads = [
        pltpu.make_async_copy(src, dst, load.at[index])
        for index, (src, dst) in enumerate(
            (
                (q_ref, qg.at[mine, low]), (g_ref, qg.at[mine, high]), (k_ref, kg.at[mine, low]),
                (v_ref, kg.at[mine, high]), (a_ref, own_a), (l_ref, own_l),
            )
        )
    ]
    for copy in loads:
        copy.start()
    for copy in loads:
        copy.wait()
    pl.semaphore_wait(barrier, len(others))

    def key_rows(block, count):
        return pl.ds((block // 4) * 2 * LEVEL + (block % 4) * H, count * H)

    def send_rows(name, src, dst, count, to):
        start(
            name, qg.at[pl.ds(src * H, count * H), main], qg.at[pl.ds(dst * H, count * H), main], to
        )

    def send_stats(name, src, dst, count, to):
        start(name + "s", qs.at[pl.ds(src, count)], qs.at[pl.ds(dst, count)], to)

    def send_keys(name, src, dst, count, to):
        start(name, kg.at[key_rows(src, count), main], kg.at[key_rows(dst, count), main], to)

    def share_keys(level):
        here, there = level * 2 * LEVEL, (level * 2 + 1) * LEVEL
        start(f"c{level}", kg.at[pl.ds(here, LEVEL), main], kg.at[pl.ds(there, LEVEL), main], sibling)

    def hand_on(slot, count):
        send_rows(f"qx{slot}", OWN[slot], PAIR[slot], count, q_pair)
        send_keys(f"kx{slot}", OWN[slot], PAIR[slot], count, k_pair)

    def send_on(slot, way):
        send_rows(f"q{slot + 2}", OWN[slot], OWN[slot + 2], 1, z_ring(way))
        send_keys(f"k{slot + 2}", OWN[slot], OWN[slot + 2], 1, y_ring(way))
        half = H // 2
        low = 0 if way > 0 else half
        there = pl.ds(OWN[7] * H + low, half)
        start(f"q7{way}", qg.at[pl.ds(OWN[slot] * H + low, half), main], qg.at[there, main], z_ring(2 * way))
        here, there = key_rows(OWN[slot], 1).start + low, key_rows(OWN[7], 1).start + low
        start(f"k7{way}", kg.at[pl.ds(here, half), main], kg.at[pl.ds(there, half), main], y_ring(2 * way))

    def hand_stats(slot, count):
        arrived(*(f"q{slot + index}s" for index in range(count)))
        send_stats(f"qx{slot}", OWN[slot], PAIR[slot], count, q_pair)

    def came(*slots):
        for slot in slots:
            arrived(f"q{slot}", f"k{slot}")

    def handed(*slots):
        for slot in slots:
            arrived(f"qx{slot}", f"kx{slot}")

    def to_ring(slot):
        send_rows(f"q{slot}", 0, OWN[slot], 1, z_ring(-OFFSETS[slot]))
        send_keys(f"k{slot}", 0, OWN[slot], 1, y_ring(-OFFSETS[slot]))

    to_ring(1)
    to_ring(2)
    send_rows("qx0", 0, PAIR[0], 1, q_pair)
    send_keys("kx0", 0, PAIR[0], 1, k_pair)
    to_ring(3)
    to_ring(4)

    product = qg[mine, high].astype(F32) * own_a[...].astype(F32)
    delta = jnp.sum(product.T, axis=0, keepdims=True)
    line = lax.broadcasted_iota(jnp.int32, (16, H), 0)
    stats = jnp.zeros((16, H), F32)
    for at, row in enumerate((*thirds(own_l[...] * (H**0.5)), *thirds(delta))):
        stats = jnp.where(line == at, row, stats)
    qs[0] = stats.astype(BF16)
    for slot in range(1, 8):
        send_stats(f"q{slot}", 0, OWN[slot], 1, z_ring(-OFFSETS[slot]))
    send_stats("qx0", 0, PAIR[0], 1, q_pair)

    lane = lax.broadcasted_iota(jnp.int32, (LEVEL, H), 1)
    minus = jnp.where(lane < 3, -1.0, 0.0).astype(BF16)

    def clear(column, _):
        rows = pl.ds(pl.multiple_of(column * LEVEL, LEVEL), LEVEL)
        kg[rows, 0:H] = minus
        kg[rows, 3 * H : 4 * H] = minus
        dk[:, rows] = jnp.zeros((H, LEVEL), F32)
        dv[:, rows] = jnp.zeros((H, LEVEL), F32)
        some = pl.ds(pl.multiple_of(column * 2 * H, 2 * H), 2 * H)
        dq[some, :] = jnp.zeros((2 * H, H), F32)

    lax.fori_loop(0, 8, clear, None)

    spread_at = lax.broadcasted_iota(jnp.int32, (16, H), 1)
    spread_l = jnp.where((line == spread_at) & (line < 3), 1.0, 0.0).astype(BF16)
    spread_d = jnp.where((line == spread_at + 3) & (line < 6), 1.0, 0.0).astype(BF16)

    def prepare(level):
        for block in range(4 * level, 4 * level + 4):
            rows = pl.ds(block * H, H)
            these = qs[block]
            qg[rows, 0:H] = dot(these, spread_l, 0, 0).astype(BF16)
            qg[rows, 3 * H : 4 * H] = dot(these, spread_d, 0, 0).astype(BF16)

    def grads_of(rows, keys, p, d):
        probs = jnp.exp2(dot(qg[rows, 0 : 2 * H], kg[keys, 0 : 2 * H], 1, 1) * (scale * LOG2E))
        shifted = dot(qg[rows, 2 * H : 4 * H], kg[keys, 2 * H : 4 * H], 1, 1)
        d[...] = (probs * shifted).astype(BF16)
        p[...] = probs.astype(BF16)
        dv[:, keys] += dot(qg[rows, 2 * H : 3 * H], p[...], 0, 0)
        dk[:, keys] += dot(qg[rows, H : 2 * H], d[...], 0, 0)
        dq[rows, :] += dot(d[...], kg[keys, H : 2 * H], 1, 0)

    def tiles(first, count, column):
        size = pl.ds(0, count * LEVEL)
        rows, keys = pl.ds(first * LEVEL, count * LEVEL), pl.ds(column * LEVEL, LEVEL)
        grads_of(rows, keys, pb.at[size], db.at[size])

    def wide(first, level):
        grads_of(pl.ds(first * LEVEL, LEVEL), pl.ds(level * 2 * LEVEL, 2 * LEVEL), pw, dw)

    came(1, 2)
    hand_on(1, 2)
    hand_stats(1, 2)
    handed(0)
    share_keys(0)
    arrived("qx0s")
    prepare(0)
    tiles(0, 1, 0)
    came(3, 4)
    send_on(3, 1)
    send_on(4, -1)
    hand_on(3, 2)
    hand_stats(3, 2)
    arrived("c0")
    tiles(0, 1, 1)
    handed(1)
    share_keys(1)
    arrived("qx1s")
    prepare(1)
    hand_stats(5, 2)
    hand_stats(7, 1)
    wide(1, 0)
    came(5, 6)
    hand_on(5, 2)
    arrived("q71", "q7-1", "k71", "k7-1")
    hand_on(7, 1)
    tiles(0, 2, 2)
    arrived("c1")
    tiles(0, 2, 3)
    handed(3)
    share_keys(2)
    arrived("qx3s")
    prepare(2)
    tiles(0, 3, 4)
    arrived("c2")
    tiles(0, 3, 5)
    handed(5, 7)
    share_keys(3)
    arrived("qx5s", "qx7s")
    prepare(3)
    wide(2, 1)

    def swap(level):
        theirs = pl.ds((2 * level + 1) * LEVEL, LEVEL)
        c_out[level, 0] = dk[:, theirs].astype(BF16)
        c_out[level, 1] = dv[:, theirs].astype(BF16)
        start(f"s{level}", c_out.at[level], c_in.at[level], sibling)

    def key_sum(which, block, count):
        grads = (dk, dv)[which]
        level, part = block // 4, pl.ds((block % 4) * H, count * H)
        here = pl.ds(level * 2 * LEVEL + (block % 4) * H, count * H)
        return grads[:, here] + c_in[level, which, :, part].astype(F32)

    def slots(first, count):
        return pl.ds(first * H, count * H)

    def keys_to_pair(first, count):
        part = slots(first, count)
        for which in range(2):
            kx_out[which, :, part] = key_sum(which, PAIR[first], count).astype(BF16)
        start(f"dkx{first}", kx_out.at[:, :, part], kx_in.at[:, :, part], k_pair)

    def key_total(which, slot):
        total = key_sum(which, OWN[slot], 1) + kx_in[which, :, slots(slot, 1)].astype(F32)
        if slot in (3, 4) and which == 4 - slot:
            total += k_in[7, which].astype(F32)
        return total

    def keys_to_owner(slot):
        for which in range(2):
            k_out[slot, which] = key_total(which, slot).astype(BF16)
        if slot == 7:
            for which, to in enumerate((2, -2)):
                start(f"dk7{which}", k_out.at[7, which], k_in.at[7, which], y_ring(to))
        else:
            start(f"dk{slot}", k_out.at[slot], k_in.at[slot], y_ring(OFFSETS[slot]))

    def queries_to_pair(first, count):
        part = slots(first, count)
        qx_out[part] = dq[slots(PAIR[first], count), :].astype(BF16)
        start(f"dqx{first}", qx_out.at[part], qx_in.at[part], q_pair)

    def query_total(slot, low=0, count=H):
        total = dq[pl.ds(OWN[slot] * H + low, count), :]
        return total + qx_in[pl.ds(slot * H + low, count)].astype(F32)

    def queries_to_owner(slot):
        half = H // 2
        for at in range(2):
            part = pl.ds(at * half, half)
            total = query_total(slot, at * half, half)
            if slot == 4 - at:
                total += q_in[7, part].astype(F32)
            q_out[slot, part] = total.astype(BF16)
            if slot == 7:
                start(f"dq7{at}", q_out.at[7, part], q_in.at[7, part], z_ring(2 - 4 * at))
        if slot != 7:
            start(f"dq{slot}", q_out.at[slot], q_in.at[slot], z_ring(OFFSETS[slot]))

    arrived("c3")
    tiles(0, 4, 7)
    swap(3)
    tiles(0, 4, 6)
    arrived("s3")
    keys_to_pair(7, 1)
    keys_to_pair(5, 2)
    queries_to_pair(1, 2)
    queries_to_pair(0, 1)
    wide(3, 2)
    swap(2)
    wide(3, 1)
    swap(1)
    arrived("s2")
    keys_to_pair(3, 2)
    wide(3, 0)
    queries_to_pair(7, 1)
    queries_to_pair(5, 2)
    arrived("dkx7")
    keys_to_owner(7)
    arrived("dkx5")
    keys_to_owner(5)
    keys_to_owner(6)
    arrived("s1")
    keys_to_pair(1, 2)
    arrived("dqx0", "dqx1")
    queries_to_owner(1)
    queries_to_owner(2)
    wide(2, 0)
    queries_to_pair(3, 2)
    swap(0)
    arrived("dqx7")
    queries_to_owner(7)
    arrived("dqx5")
    queries_to_owner(5)
    queries_to_owner(6)
    arrived("s0")
    keys_to_pair(0, 1)
    arrived("dkx3", "dk70", "dk71")
    keys_to_owner(3)
    keys_to_owner(4)
    arrived("dqx3", "dq70", "dq71")
    queries_to_owner(3)
    queries_to_owner(4)
    arrived("dkx1")
    keys_to_owner(1)
    keys_to_owner(2)
    last = ("dkx0",) + tuple(f"d{kind}{slot}" for kind in "qk" for slot in range(1, 8))
    last = tuple(name for name in copies if name in last)
    for name, copy in copies.items():
        if name not in last:
            copy.wait_send()

    total = query_total(0)
    for slot in range(1, 7):
        arrived(f"dq{slot}")
        total += q_in[slot].astype(F32)
    out_ref[0] = (total * scale).astype(BF16)
    arrived("dkx0")
    for slot in range(1, 7):
        arrived(f"dk{slot}")
    for which, by in enumerate((scale, 1.0)):
        total = key_total(which, 0)
        for slot in range(1, 7):
            total += k_in[slot, which].astype(F32)
        out_ref[1 + which] = (total * by).T.astype(BF16)
    for name in last:
        copies[name].wait_send()


def part(grads, *outs):
    for index, out in enumerate(outs):
        out[...] = grads[index]


COPIES = 80


def shards(queries, keys, values, attended, out_grad, logsumexp):
    vmem = pl.BlockSpec(memory_space=pltpu.VMEM)
    block = jax.ShapeDtypeStruct((H, H), BF16)
    keys_shape = pltpu.VMEM((2, H, 8 * H), BF16)
    grads = pl.pallas_call(
        kernel,
        out_shape=jax.ShapeDtypeStruct((3, H, H), BF16),
        in_specs=[pl.BlockSpec(memory_space=pl.ANY)] * 6,
        out_specs=vmem,
        scratch_shapes=[
            pltpu.VMEM((H, H), BF16),
            pltpu.VMEM((1, H), F32),
            pltpu.SemaphoreType.DMA((6,)),
            pltpu.VMEM((LEVEL, 2 * LEVEL), BF16),
            pltpu.VMEM((LEVEL, 2 * LEVEL), BF16),
            pltpu.VMEM((4 * LEVEL, 4 * H), BF16),
            pltpu.VMEM((16, 16, H), BF16),
            pltpu.VMEM((8 * LEVEL, 4 * H), BF16),
            pltpu.VMEM((4 * LEVEL, H), F32),
            pltpu.VMEM((H, 8 * LEVEL), F32),
            pltpu.VMEM((H, 8 * LEVEL), F32),
            pltpu.VMEM((4 * LEVEL, LEVEL), BF16),
            pltpu.VMEM((4 * LEVEL, LEVEL), BF16),
            pltpu.VMEM((4, 2, H, LEVEL), BF16),
            pltpu.VMEM((4, 2, H, LEVEL), BF16),
            keys_shape,
            keys_shape,
            pltpu.VMEM((8, 2, H, H), BF16),
            pltpu.VMEM((8, 2, H, H), BF16),
            pltpu.VMEM((8 * H, H), BF16),
            pltpu.VMEM((8 * H, H), BF16),
            pltpu.VMEM((8, H, H), BF16),
            pltpu.VMEM((8, H, H), BF16),
            pltpu.SemaphoreType.DMA((COPIES,)),
            pltpu.SemaphoreType.DMA((COPIES,)),
        ],
        compiler_params=pltpu.CompilerParams(
            collective_id=0, has_side_effects=True, vmem_limit_bytes=56 * 2**20
        ),
    )(queries, keys, values, attended, out_grad, logsumexp.reshape(1, H))
    return pl.pallas_call(
        part, out_shape=(block, block, block), in_specs=[vmem], out_specs=[vmem] * 3
    )(grads)


def solution(mesh):
    rows, flat = P(("outer", "inner"), None), P(("outer", "inner"))
    return jax.shard_map(
        shards,
        mesh=mesh,
        in_specs=(rows, rows, rows, rows, rows, flat),
        out_specs=(rows, rows, rows),
        check_vma=False,
    )
```

time: 68.3 us -> 63.1 us (0.924)
  local copies, waits for them, and re-layouts: 2.77 us -> 0 us
  Pallas kernels: 64.6 us -> 62.3 us
    unnamed x7 -> x0, local copies, waits for them, and re-layouts: 2.77 us -> none
    pallas_call x1 -> x2, Pallas kernels: 64.6 us -> 62.3 us  [the longest x1 60.7 us: shards(): pl.pallas_call(kernel, out_shape=jax.ShapeDtypeStruct((3, H, H), BF16), i...]
where the time goes in v4:
time: 63.1 us; the launch traced here: 62.9 us
  Pallas kernels  62.3 us (99%)
  between operations  0.64 us (1%)
    pallas_call x1, Pallas kernels, shards(): pl.pallas_call(kernel, out_shape=jax.ShapeDtypeStruct((3, H, H), BF16), i...  60.7 us
    pallas_call x1, Pallas kernels, shards(): pl.pallas_call(part, out_shape=(block, block, block), in_specs=[vmem], ou...  1.53 us

profile of v4, /device:TPU:1, one launch (start us, length us, event | category | flops | bytes accessed | tf_op | source)
XLA Modules:
  0.0 62.9 jit_solution(7980767323861287621)
XLA Ops:
  0.6 60.7 %shard_map.85.grads = bf16[3,128,128]{2,1,0:T(8,128)(2,1)} custom-call(bf16[128,128]{1,0:T(8,128)(2,1)} %q_ref.1, bf16[128,128]{1,0:T(8,128)(2,1)} %k_ref.1, bf16[128,128]{1,0:T(8,128)(2,1)} %v_ref.1, bf16[128,128]{1,0:T(8,128)(2,1)} %a_ref.1, bf16[128,128]{1,0:T(8,128)(2,1)} %g_ref.1, f32[1,128]{1,0:T(1,128)} %bitcast.1), custom_call_target="tpu_custom_call" | custom-call | tf_op jit(solution)/shard_map/pallas_call | solution.py:386
  61.4 1.5 %shard_map.86 = (bf16[128,128]{1,0:T(8,128)(2,1)}, bf16[128,128]{1,0:T(8,128)(2,1)}, bf16[128,128]{1,0:T(8,128)(2,1)}) custom-call(bf16[3,128,128]{2,1,0:T(8,128)(2,1)} %shard_map.85.grads), custom_call_target="tpu_custom_call" | custom-call | tf_op jit(solution)/shard_map/pallas_call | solution.py:422

commit v5 on v4

--- a/solution.py
+++ b/solution.py
@@ -371,9 +371,16 @@
         copies[name].wait_send()
 
 
-def part(grads, *outs):
-    for index, out in enumerate(outs):
-        out[...] = grads[index]
+def part(grads, *refs):
+    *outs, done = refs
+    copies = [
+        pltpu.make_async_copy(grads.at[index], out, done.at[index])
+        for index, out in enumerate(outs)
+    ]
+    for copy in copies:
+        copy.start()
+    for copy in copies:
+        copy.wait()
 
 
 COPIES = 80
@@ -420,7 +427,11 @@
         ),
     )(queries, keys, values, attended, out_grad, logsumexp.reshape(1, H))
     return pl.pallas_call(
-        part, out_shape=(block, block, block), in_specs=[vmem], out_specs=[vmem] * 3
+        part,
+        out_shape=(block, block, block),
+        in_specs=[pl.BlockSpec(memory_space=pl.ANY)],
+        out_specs=[pl.BlockSpec(memory_space=pl.ANY)] * 3,
+        scratch_shapes=[pltpu.SemaphoreType.DMA((3,))],
     )(grads)
 
 

time: 63.1 us -> 65.8 us (1.043)
  Pallas kernels: 62.3 us -> 64.8 us
    pallas_call x1, Pallas kernels: 1.53 us -> 4.11 us  [shards(): pl.pallas_call(part, out_shape=(block, block, block), in_specs=[pl.BlockS...]
where the time goes in v5:
time: 65.8 us; the launch traced here: 65.6 us
  Pallas kernels  64.8 us (98%)
  between operations  0.8 us (1%)
    pallas_call x1, Pallas kernels, shards(): pl.pallas_call(kernel, out_shape=jax.ShapeDtypeStruct((3, H, H), BF16), i...  60.7 us
    pallas_call x1, Pallas kernels, shards(): pl.pallas_call(part, out_shape=(block, block, block), in_specs=[pl.BlockS...  4.11 us

profile of v5, /device:TPU:1, one launch (start us, length us, event | category | flops | bytes accessed | tf_op | source)
XLA Modules:
  0.0 65.6 jit_solution(3709923314215486923)
XLA Ops:
  0.6 60.7 %shard_map.85.grads = bf16[3,128,128]{2,1,0:T(8,128)(2,1)} custom-call(bf16[128,128]{1,0:T(8,128)(2,1)} %q_ref.1, bf16[128,128]{1,0:T(8,128)(2,1)} %k_ref.1, bf16[128,128]{1,0:T(8,128)(2,1)} %v_ref.1, bf16[128,128]{1,0:T(8,128)(2,1)} %a_ref.1, bf16[128,128]{1,0:T(8,128)(2,1)} %g_ref.1, f32[1,128]{1,0:T(1,128)} %bitcast.1), custom_call_target="tpu_custom_call" | custom-call | tf_op jit(solution)/shard_map/pallas_call | solution.py:393
  61.4 4.1 %shard_map.86 = (bf16[128,128]{1,0:T(8,128)(2,1)}, bf16[128,128]{1,0:T(8,128)(2,1)}, bf16[128,128]{1,0:T(8,128)(2,1)}) custom-call(bf16[3,128,128]{2,1,0:T(8,128)(2,1)} %shard_map.85.grads), custom_call_target="tpu_custom_call" | custom-call | tf_op jit(solution)/shard_map/pallas_call | solution.py:429
